TPU v7x, 512 devices: a whole 4x4x16 slice. The times are simulated.
512 devices in a mesh: seq: 128 (over z, x, core), head: 4 (over y).
Axes of the slice: x: 4, y: 4, z: 16, core: 2. Of those that a mesh axis runs over, the one named last changes fastest.
Arguments:
- queries: bfloat16 [65536, 2048], P('seq', 'head'), may hold values from -6 to 6
- keys: bfloat16 [65536, 2048], P('seq', 'head'), may hold values from -6 to 6
- values: bfloat16 [65536, 2048], P('seq', 'head'), may hold values from -6 to 6
- grad_out: bfloat16 [65536, 2048], P('seq', 'head'), may hold values from -24 to 24
- out_weight: bfloat16 [2048, 2048], P('seq', 'head'), may hold values from -0.125 to 0.125
Outputs:
- query_grad: bfloat16 [65536, 2048], P('seq', 'head')
- key_grad: bfloat16 [65536, 2048], P('seq', 'head')
- value_grad: bfloat16 [65536, 2048], P('seq', 'head')
- weight_grad: float32 [2048, 2048], P('seq', 'head')
All inputs are finite; a program needn't handle non-finite values.
Results may differ from a plain program's by a relative error of at most 0.0057.
Values may be sent and summed in bfloat16 or wider, within the bound.
A program may use at most 192 MiB of HBM per device.

v0:
```python
import math

import jax
import jax.numpy as jnp
from jax import lax
from jax.sharding import PartitionSpec as P

HEAD_DIM = 128


def entering(x, axis, combine, identity, reverse):
    length, position = (lax.axis_size(axis), lax.axis_index(axis))
    everything = lax.all_gather(x, axis)
    start = jnp.broadcast_to(jnp.asarray(identity, x.dtype), x.shape)

    def hop(k, before):
        at = length - 1 - k if reverse else k
        reached = at > position if reverse else at < position
        new = combine(before, everything[at])
        return jnp.where(reached, new, before)

    return lax.fori_loop(0, length, hop, start)


def add_one(earlier, later):
    return earlier + later


def per_device(queries, keys, values, grad_out, out_weight):
    seq_count = lax.axis_size("seq")
    tok_rows, width = queries.shape
    heads = width // HEAD_DIM
    total_tokens = tok_rows * seq_count
    scale = 1.0 / math.sqrt(HEAD_DIM * total_tokens)
    grads_full = lax.all_gather(grad_out, "head", axis=1, tiled=True)
    weight_full = lax.all_gather(out_weight, "seq", axis=0, tiled=True)
    attn_grad = jnp.dot(grads_full, weight_full, preferred_element_type=jnp.float32).astype(
        jnp.bfloat16
    )
    q_heads = queries.reshape(tok_rows, heads, HEAD_DIM)
    k_heads = keys.reshape(tok_rows, heads, HEAD_DIM)
    v_heads = values.reshape(tok_rows, heads, HEAD_DIM)
    g_heads = attn_grad.reshape(tok_rows, heads, HEAD_DIM)
    kv_own = jnp.einsum("thi,thj->hij", k_heads, v_heads, preferred_element_type=jnp.float32)
    qg_own = jnp.einsum("thi,thj->hij", q_heads, g_heads, preferred_element_type=jnp.float32)
    zeros_state = jnp.zeros_like(kv_own)
    kv_prev = entering(kv_own, "seq", add_one, zeros_state, False)
    qg_next = entering(qg_own, "seq", add_one, zeros_state, True)
    prefix = kv_prev.astype(jnp.bfloat16)
    suffix = qg_next.astype(jnp.bfloat16)
    causal = jnp.tril(jnp.ones((tok_rows, tok_rows), bool))
    attn = jnp.where(
        causal[None],
        jnp.einsum("thi,shi->hts", q_heads, k_heads, preferred_element_type=jnp.float32),
        0.0,
    ).astype(jnp.bfloat16)
    back = jnp.where(
        causal[None],
        jnp.einsum("thj,shj->hts", g_heads, v_heads, preferred_element_type=jnp.float32),
        0.0,
    ).astype(jnp.bfloat16)
    out_rec = scale * (
        jnp.einsum("hts,shj->thj", attn, v_heads, preferred_element_type=jnp.float32)
        + jnp.einsum("thi,hij->thj", q_heads, prefix, preferred_element_type=jnp.float32)
    )
    out_flat = out_rec.astype(jnp.bfloat16).reshape(tok_rows, width)
    q_grad = scale * (
        jnp.einsum("hts,shi->thi", back, k_heads, preferred_element_type=jnp.float32)
        + jnp.einsum("thj,hij->thi", g_heads, prefix, preferred_element_type=jnp.float32)
    )
    k_grad = scale * (
        jnp.einsum("hts,thi->shi", back, q_heads, preferred_element_type=jnp.float32)
        + jnp.einsum("shj,hij->shi", v_heads, suffix, preferred_element_type=jnp.float32)
    )
    v_grad = scale * (
        jnp.einsum("hts,thj->shj", attn, g_heads, preferred_element_type=jnp.float32)
        + jnp.einsum("shi,hij->shj", k_heads, suffix, preferred_element_type=jnp.float32)
    )
    weight_grad = lax.psum_scatter(
        lax.dot_general(
            grads_full, out_flat, (((0,), (0,)), ((), ())), preferred_element_type=jnp.float32
        ),
        "seq",
        scatter_dimension=0,
        tiled=True,
    ) * (1.0 / math.sqrt(total_tokens))
    return (
        q_grad.astype(jnp.bfloat16).reshape(tok_rows, width),
        k_grad.astype(jnp.bfloat16).reshape(tok_rows, width),
        v_grad.astype(jnp.bfloat16).reshape(tok_rows, width),
        weight_grad,
    )


def solution(mesh):
    in_specs = (
        P("seq", "head"),
        P("seq", "head"),
        P("seq", "head"),
        P("seq", "head"),
        P("seq", "head"),
    )
    out_specs = (P("seq", "head"), P("seq", "head"), P("seq", "head"), P("seq", "head"))
    return jax.shard_map(
        per_device, mesh=mesh, in_specs=in_specs, out_specs=out_specs, check_vma=False
    )
```

profile of v0, /device:TPU:8, one launch (start us, length us, event | category | flops | bytes accessed | tf_op | source)
XLA Modules:
  0.0 860.1 jit_solution(12573711937423579405)
XLA Ops:
  8.7 1.3 copy.57
  10.0 2.1 fusion.15
  12.1 40.0 %all-gather.7.cloned.1.call-done = bf16[512,2048]{1,0:T(8,128)(2,1)} async-done(((bf16[512,512]{1,0:T(8,128)(2,1)}), bf16[512,2048]{1,0:T(8,128)(2,1)}) %all-gather.7.cloned.1.call-update) | async-done | bytes 2097168 | tf_op jit(solution)/shard_map/all_gather | solution.py:35
  52.1 144.0 %all-gather.9.cloned.1.call-done = bf16[2048,512]{1,0:T(8,128)(2,1)} async-done(((bf16[16,512]{1,0:T(8,128)(2,1)}), bf16[2048,512]{1,0:T(8,128)(2,1)}) %all-gather.9.cloned.1.call-update) | async-done | bytes 2097168 | tf_op jit(solution)/shard_map/all_gather | solution.py:36
  196.1 3.5 convolution_convert_fusion
  201.7 1.8 convolution_bitcast_fusion.2
  204.3 1.5 convolution_bitcast_fusion.1
  205.8 1.8 convolution_bitcast_fusion.3
  207.6 1.4 fusion.32
  209.1 182.3 %all-gather.11.cloned.1.call-done = f32[512,128,128]{2,1,0:T(8,128)} async-done(((f32[4,128,128]{2,1,0:T(8,128)}), f32[512,128,128]{2,1,0:T(8,128)}) %all-gather.11.cloned.1.call-update) | async-done | bytes 33554448 | tf_op jit(solution)/shard_map/all_gather | solution.py:13
  391.3 136.7 %while.30 = (s32[]{:T(128)}, f32[4,128,128]{2,1,0:T(8,128)S(1)}, s32[]{:T(128)}, f32[128,4,128,128]{3,2,1,0:T(8,128)}, s32[]{:T(128)}, /*index=5*/s32[]{:T(128)}) while((s32[]{:T(128)}, f32[4,128,128]{2,1,0:T(8,128)S(1)}, s32[]{:T(128)}, f32[128,4,128,128]{3,2,1,0:T(8,128)}, s32[]{:T(128)}, /*index=5*/s32[]{:T(128)}) %tuple.91), condition=%wide.region_1.2_spmd.clone, body=%wide.region_0.1_spmd.clone.sunk | while | flops 196612 | bytes 786533 | solution.py:22
  413.7 1.0 add_select_fusion.4
  479.7 1.1 add_select_fusion.4
  480.9 1.1 add_select_fusion.4
  482.0 1.1 add_select_fusion.4
  489.4 1.1 add_select_fusion.4
  494.8 1.1 add_select_fusion.4
  501.2 1.0 add_select_fusion.4
  506.6 1.1 add_select_fusion.4
  507.7 1.1 add_select_fusion.4
  516.2 1.1 add_select_fusion.4
  520.5 1.1 add_select_fusion.4
  524.8 1.1 add_select_fusion.4
  527.0 1.1 add_select_fusion.4
  528.1 1.6 fusion.7
  530.6 1.8 fusion.10
  532.6 3.3 convolution_bitcast_fusion
  535.9 5.5 copy.55
  541.4 45.1 %all-gather.13.cloned.1.call-done = f32[512,128,128]{2,1,0:T(8,128)} async-done(((f32[4,128,128]{2,1,0:T(8,128)}), f32[512,128,128]{2,1,0:T(8,128)}) %all-gather.13.cloned.1.call-update) | async-done | bytes 33554448 | tf_op jit(solution)/shard_map/all_gather | solution.py:13
  586.5 137.0 %while.31 = (s32[]{:T(128)}, f32[4,128,128]{2,1,0:T(8,128)S(1)}, s32[]{:T(128)}, f32[128,4,128,128]{3,2,1,0:T(8,128)}, s32[]{:T(128)}, /*index=5*/s32[]{:T(128)}, s32[]{:T(128)}, s32[]{:T(128)}) while((s32[]{:T(128)}, f32[4,128,128]{2,1,0:T(8,128)S(1)}, s32[]{:T(128)}, f32[128,4,128,128]{3,2,1,0:T(8,128)}, s32[]{:T(128)}, ...), condition=%wide.region_3.4_spmd.clone, body=%wide.region_2.3_spmd.clone.sunk | while | flops 196616 | bytes 786595 | solution.py:22
  723.6 1.6 fusion.8
  727.6 124.4 %reduce-scatter.4.cloned.1.call-done = f32[16,512]{1,0:T(8,128)} async-done(((f32[2048,512]{1,0:T(8,128)}), f32[16,512]{1,0:T(8,128)}) %reduce-scatter.4.cloned.1.call-update) | async-done | bytes 32784
  (275 shorter events, 262.8 us)
Async XLA Ops:
  7.2 192.5 %copy-start = (bf16[512,512]{1,0:T(8,128)(2,1)S(1)}, bf16[512,512]{1,0:T(8,128)(2,1)}, u32[]{:S(2)}) copy-start(bf16[512,512]{1,0:T(8,128)(2,1)} %param.9) | copy-start | bytes 1572868
  7.2 44.9 %all-gather.7.cloned.1.call-start = ((), (), s32[]{:S(2)}) async-start(), calls=%async_computation.1 | async-start | bytes 2621440 | tf_op jit(solution)/shard_map/all_gather | solution.py:35
  7.9 188.2 %all-gather.9.cloned.1.call-start = ((), (), s32[]{:S(2)}) async-start(), calls=%async_computation.2 | async-start | bytes 2113536 | tf_op jit(solution)/shard_map/all_gather | solution.py:36
  8.7 382.7 %all-gather.11.cloned.1.call-start = ((), (), s32[]{:S(2)}) async-start(), calls=%async_computation.3 | async-start | bytes 33816576 | tf_op jit(solution)/shard_map/all_gather | solution.py:13
  12.1 574.4 %all-gather.13.cloned.1.call-start = ((), (), s32[]{:S(2)}) async-start(), calls=%async_computation.4 | async-start | bytes 33816576 | tf_op jit(solution)/shard_map/all_gather | solution.py:13
  199.6 1.4 copy-start.1
  200.8 651.1 %reduce-scatter.4.cloned.1.call-start = ((), (), s32[]{:S(2)}) async-start(), calls=%async_computation.5 | async-start | bytes 4227072
  530.6 2.0 copy-start.3
  723.6 2.6 copy-start.2
Sparse Core Ops, SparseCore 0:
  10.1 41.9 all-gather.6
  55.2 140.7 all-gather.8
  199.8 191.4 all-gather.10
  394.9 191.5 all-gather.12
  591.0 260.8 reduce-scatter.3
where the time goes:
time: 868 us; the launch traced here: 860 us
  waiting for transfers between devices  537 us (62%)
  other arithmetic  267 us (31%)
  matrix products  22.5 us (3%)
  between operations  13.9 us (2%)
  local copies, waits for them, and re-layouts  12.4 us (1%)
    select_n x256, other arithmetic, hop(): return jnp.where(reached, new, before)  267 us
    all_gather x2, waiting for transfers between devices, entering(): everything = lax.all_gather(x, axis)  227 us
    all_gather x1, waiting for transfers between devices, per_device(): weight_full = lax.all_gather(out_weight, 'seq', axis=0, tiled=True)  144 us
    unnamed x6, waiting for transfers between devices  126 us
    all_gather x1, waiting for transfers between devices, per_device(): grads_full = lax.all_gather(grad_out, 'head', axis=1, tiled=True)  40 us
  transfers between devices with their start and end apart: 5, of which 5 were waited for; matrix products, arithmetic and copies ran while one was open for 35% of the time, Pallas kernels for 0%

commit v1 on v0

v1 whole, which is shorter than its diff:
```python
import math

import jax
import jax.numpy as jnp
from jax import lax
from jax.experimental import pallas as pl
from jax.experimental.pallas import tpu as pltpu
from jax.sharding import PartitionSpec as P

MESH = pl.DeviceIdType.MESH
F32, BF16 = jnp.float32, jnp.bfloat16
D = 128
T = 512
SCALE = 1.0 / math.sqrt(128 * 65536)
WSCALE = 1.0 / math.sqrt(65536)


def dot_nn(a, b):
    return lax.dot_general(a, b, (((1,), (0,)), ((), ())), preferred_element_type=F32)


def dot_nt(a, b):
    return lax.dot_general(a, b, (((1,), (1,)), ((), ())), preferred_element_type=F32)


def dot_tn(a, b):
    return lax.dot_general(a, b, (((0,), (0,)), ((), ())), preferred_element_type=F32)


def heads(body):
    def step(h, carry):
        body(h, pl.ds(pl.multiple_of(h * D, D), D))
        return carry

    lax.fori_loop(0, 4, step, 0)


def times(low, high, body):
    def step(i, carry):
        body(i)
        return carry

    lax.fori_loop(low, high, step, 0)


def kernel(
    q_in, k_in, v_in, g_in, w_in,
    q_out, k_out, v_out, w_out,
    q, k, v, gbuf, wown, wst, av, outb, agf, ag, kpart, vpart,
    sb, s1, s2s, s2, s3s, state,
    hf, rs, r1, hb, r2, h2, h2b, r3, h3, ra, fin, rc,
    wo,
    load_sem, store_sem,
    g_ss, g_rs, w0_ss, w0_rs, wa_ss, wa_rs, w2_ss, w2_rs, w3_ss, w3_rs, w4_ss, w4_rs,
    p1_ss, p1_rs, p2_ss, p2_rs, p3_ss, p3_rs,
    r1_ss, r1_rs, r2_ss, r2_rs, r3_ss, r3_rs, ra_ss, ra_rs, rc_ss, rc_rs,
):
    seq = lax.axis_index("seq")
    y = lax.axis_index("head")
    z, x, c = seq // 8, (seq // 2) % 4, seq % 2
    zq, zr = z // 4, z % 4
    group, m = seq // 16, seq % 16
    oc = 1 - c
    a2 = oc * zr + c * x
    a3 = oc * x + c * zr
    zstep = (0, 1, 2, 15)

    def dev(z_, x_, c_):
        return ((z_ * 4 + x_) * 2 + c_, y)

    def along(first, n):
        return dev(first * ((z + zstep[n]) % 16) + (1 - first) * z, first * x + (1 - first) * ((x + n) % 4), c)

    def peer2(n):
        return along(oc, n)

    def peer3(n):
        return along(c, n)

    def peer4(n):
        return dev((z + 4 * n) % 16, x, c)

    other = dev(z, x, oc)

    def remote(src, dst, ss, rs_, to):
        return pltpu.make_async_remote_copy(
            src_ref=src, dst_ref=dst, send_sem=ss, recv_sem=rs_, device_id=to, device_id_type=MESH
        )

    loads = [
        pltpu.make_async_copy(src, dst, load_sem.at[i])
        for i, (src, dst) in enumerate(((k_in, k), (v_in, v), (w_in, wown), (q_in, q), (g_in, gbuf.at[y])))
    ]
    for copy in loads:
        copy.start()

    barrier = pltpu.get_barrier_semaphore()

    def greet(to):
        pl.semaphore_signal(barrier, inc=1, device_id=to, device_id_type=MESH)

    times(1, 16, lambda n: greet((group * 16 + (m + n) % 16, y)))
    times(1, 8, lambda n: greet((((group + n) % 8) * 16 + m, y)))
    times(1, 4, lambda n: greet((seq, (y + n) % 4)))
    greet(dev((z + 1) % 16, x, c))
    greet(dev((z + 15) % 16, x, c))
    pl.semaphore_wait(barrier, 27)

    def g_copy(n):
        return remote(g_in, gbuf.at[y], g_ss.at[n - 1], g_rs.at[n - 1], (seq, (y + n) % 4))

    for n in (1, 3, 2):
        g_copy(n).start()

    loads[2].wait()
    w0 = remote(
        wown.at[:, pl.ds(pl.multiple_of(oc * 256, 256), 256)],
        wst.at[oc, zq, a2, a3, c],
        w0_ss, w0_rs, other,
    )
    w0.start()
    wst[c, zq, a3, a2, c] = wown[:, pl.ds(pl.multiple_of(c * 256, 256), 256)]

    loads[0].wait()
    loads[1].wait()

    def scan_piece1(i, n):
        to = (m + n) % 16
        return remote(sb.at[i, to], s1.at[i, m], p1_ss.at[i, n - 1], p1_rs.at[i, n - 1], (group * 16 + to, y))

    def scan_piece2(i, n):
        return remote(s2s.at[i], s2.at[i, group], p2_ss.at[i, n - 1], p2_rs.at[i, n - 1], (((group + n) % 8) * 16 + m, y))

    def scan_piece3(i, n):
        to = (m + n) % 16
        return remote(s3s.at[i, to], state.at[i, m], p3_ss.at[i, n - 1], p3_rs.at[i, n - 1], (group * 16 + to, y))

    def scan_send(i, a, b):
        def one(h, cols):
            s = dot_tn(a[:, cols], b[:, cols]).astype(BF16)
            sb[i, pl.ds(h * 4, 4)] = s.reshape(4, 32, D)

        heads(one)
        times(1, 16, lambda n: scan_piece1(i, n).start())
        s1[i, m] = sb[i, m]

    def scan_total(i):
        times(1, 16, lambda n: scan_piece1(i, n).wait_recv())
        total = s1[i, 0].astype(F32)
        for j in range(1, 16):
            total += s1[i, j].astype(F32)
        s2s[i] = total.astype(s2s.dtype)
        times(1, 8, lambda n: scan_piece2(i, n).start())
        s2[i, group] = jnp.zeros_like(s2[i, group])

    def scan_back(i):
        times(1, 8, lambda n: scan_piece2(i, n).wait_recv())
        run = jnp.zeros((32, D), F32)
        for j in range(8):
            counts = (j < group) if i == 0 else (j > group)
            run += jnp.where(counts, s2[i, j].astype(F32), 0.0)
        for j in range(16) if i == 0 else range(15, -1, -1):
            s3s[i, j] = run.astype(BF16)
            run += s1[i, j].astype(F32)
        times(1, 16, lambda n: scan_piece3(i, n).start())
        state[i, m] = s3s[i, m]

    def scan_get(i):
        times(1, 16, lambda n: scan_piece3(i, n).wait_recv())

    def state_of(i, h):
        return state[i, pl.ds(h * 4, 4)].reshape(D, D)

    scan_send(0, k, v)

    w0.wait_recv()

    def wa_copy(n):
        part = wst.at[c, zq, a3, a2]
        return remote(part, part, wa_ss.at[n - 1], wa_rs.at[n - 1], peer4(n))

    for n in (2, 1, 3):
        wa_copy(n).start()

    loads[3].wait()

    def lower(n, height):
        row = lax.broadcasted_iota(jnp.int32, (D, n), 0) + height
        col = lax.broadcasted_iota(jnp.int32, (D, n), 1)
        return row >= col

    def upper(n):
        row = lax.broadcasted_iota(jnp.int32, (D, n), 0)
        col = lax.broadcasted_iota(jnp.int32, (D, n), 1)
        return col >= row

    def attend(h, cols):
        for r in range(4):
            n = (r + 1) * D
            rows = slice(r * D, n)
            s = dot_nt(q[rows, cols], k[:n, cols])
            s = jnp.where(lower(n, r * D), s, 0.0).astype(BF16)
            av[rows, cols] = dot_nn(s, v[:n, cols])

    heads(attend)

    scan_total(0)

    def w2_copy(n):
        part = wst.at[c, :, a3, a2]
        return remote(part, part, w2_ss.at[n - 1], w2_rs.at[n - 1], peer2(n))

    def w3_copy(n):
        part = wst.at[c, :, a3]
        return remote(part, part, w3_ss.at[n - 1], w3_rs.at[n - 1], peer3(n))

    def w4_copy(n):
        part = wst.at[c, :, (a3 + n) % 4]
        return remote(part, part, w4_ss.at[n], w4_rs.at[n], other)

    for n in (1, 2, 3):
        wa_copy(n).wait_recv()
    for n in (1, 3, 2):
        w2_copy(n).start()
    for n in (1, 3, 2):
        w2_copy(n).wait_recv()
    for n in (1, 3, 2):
        w3_copy(n).start()
    w4_copy(0).start()

    scan_back(0)

    for n in (1, 3, 2):
        w3_copy(n).wait_recv()
        w4_copy((4 - n) % 4).start()

    scan_get(0)

    def rec(h, cols):
        outb[:, cols] = (SCALE * (av[:, cols] + dot_nn(q[:, cols], state_of(0, h)))).astype(BF16)

    heads(rec)

    loads[4].wait()
    for n in (1, 3, 2):
        g_copy(n).wait_recv()

    def r1_copy(i):
        return remote(rs.at[i], r1.at[i], r1_ss.at[i], r1_rs.at[i], other)

    def contribute(i):
        mine = dot_tn(gbuf[i], outb[:, pl.ds(pl.multiple_of(c * 256, 256), 256)])
        theirs = dot_tn(gbuf[i], outb[:, pl.ds(pl.multiple_of(oc * 256, 256), 256)])
        for zi in range(4):
            for xi in range(4):
                rows = slice((zi * 4 + xi) * 32, (zi * 4 + xi) * 32 + 32)
                of_x, of_z = oc * xi + c * zi, oc * zi + c * xi
                hf[i, of_x, of_z] = mine[rows].reshape(2, 16, 256)
                rs[i, of_z, of_x] = theirs[rows].reshape(2, 16, 256).astype(BF16)
        r1_copy(i).start()

    times(0, 4, contribute)

    for n in range(4):
        w4_copy(n).wait_recv()

    agf[...] = jnp.zeros_like(agf)

    def project(i):
        for half in range(2):
            order = [(xi, zi) if half == 0 else (zi, xi) for zi in range(4) for xi in range(4)]
            w = jnp.concatenate([wst[half, i, u, t].reshape(32, 256) for u, t in order], axis=0)
            agf[:, half * 256 : half * 256 + 256] += dot_nn(gbuf[i], w)

    times(0, 4, project)
    ag[...] = agf[...].astype(BF16)

    scan_send(1, q, ag)

    def r2_copy(n):
        return remote(hb.at[:, (a3 + n) % 4], r2.at[n - 1], r2_ss.at[n - 1], r2_rs.at[n - 1], peer3(n))

    def pair(i):
        r1_copy(i).wait_recv()
        for u in range(4):
            total = hf[i, u] + r1[i, u].astype(F32)
            hf[i, u] = total
            hb[i, u] = total.astype(BF16)

    times(0, 4, pair)
    for n in (1, 3, 2):
        r2_copy(n).start()

    def back(h, cols):
        for r in range(4):
            n = (r + 1) * D
            rows = slice(r * D, n)
            s = dot_nt(ag[rows, cols], v[:n, cols])
            s = jnp.where(lower(n, r * D), s, 0.0).astype(BF16)
            total = dot_nn(s, k[:n, cols]) + dot_nt(ag[rows, cols], state_of(0, h))
            outb[rows, cols] = (SCALE * total).astype(BF16)

    def back_kv(h, cols):
        for r in range(4):
            rows = slice(r * D, (r + 1) * D)
            mask = upper(T - r * D)
            s = dot_nt(v[rows, cols], ag[r * D :, cols])
            s = jnp.where(mask, s, 0.0).astype(BF16)
            kpart[rows, cols] = dot_nn(s, q[r * D :, cols])
            s = dot_nt(k[rows, cols], q[r * D :, cols])
            s = jnp.where(mask, s, 0.0).astype(BF16)
            vpart[rows, cols] = dot_nn(s, ag[r * D :, cols])

    heads(back)
    q_store = pltpu.make_async_copy(outb, q_out, store_sem.at[0])
    q_store.start()
    scan_total(1)
    heads(back_kv)

    def r3_copy(n):
        return remote(h2b.at[:, (a2 + n) % 4], r3.at[n - 1], r3_ss.at[n - 1], r3_rs.at[n - 1], peer2(n))

    for n in (1, 3, 2):
        r2_copy(n).wait_recv()

    def third(i):
        total = hf[i, a3]
        for n in range(3):
            total += r2[n, i].astype(F32)
        h2[i] = total
        h2b[i] = total.astype(BF16)

    times(0, 4, third)
    for n in (1, 3, 2):
        r3_copy(n).start()

    scan_back(1)

    def ra_copy(n):
        return remote(h3.at[(zq + n) % 4], ra.at[n - 1], ra_ss.at[n - 1], ra_rs.at[n - 1], peer4(n))

    for n in (1, 3, 2):
        r3_copy(n).wait_recv()
    for i in range(4):
        total = h2[i, a2]
        for n in range(3):
            total += r3[n, i].astype(F32)
        h3[i] = total
    for n in (2, 1, 3):
        ra_copy(n).start()

    scan_get(1)

    q_store.wait()

    def final(h, cols):
        suffix = state_of(1, h)
        outb[:, cols] = (SCALE * (kpart[:, cols] + dot_nt(v[:, cols], suffix))).astype(BF16)
        ag[:, cols] = (SCALE * (vpart[:, cols] + dot_nn(k[:, cols], suffix))).astype(BF16)

    heads(final)
    k_store = pltpu.make_async_copy(outb, k_out, store_sem.at[1])
    v_store = pltpu.make_async_copy(ag, v_out, store_sem.at[2])
    k_store.start()
    v_store.start()

    for n in (1, 2, 3):
        ra_copy(n).wait_recv()
    total = h3[zq]
    for n in range(3):
        total += ra[n]
    fin[...] = total * WSCALE
    rc_copy = remote(fin.at[oc], rc, rc_ss, rc_rs, other)
    rc_copy.start()
    wo[:, pl.ds(pl.multiple_of(c * 256, 256), 256)] = fin[c]
    rc_copy.wait_recv()
    wo[:, pl.ds(pl.multiple_of(oc * 256, 256), 256)] = rc[...]
    w_store = pltpu.make_async_copy(wo, w_out, store_sem.at[3])
    w_store.start()

    w0.wait_send()
    for n in (1, 2, 3):
        g_copy(n).wait_send()
        wa_copy(n).wait_send()
        w2_copy(n).wait_send()
        w3_copy(n).wait_send()
        r2_copy(n).wait_send()
        r3_copy(n).wait_send()
        ra_copy(n).wait_send()
    for n in range(4):
        w4_copy(n).wait_send()
    times(0, 4, lambda i: r1_copy(i).wait_send())
    for i in range(2):
        times(1, 16, lambda n, i=i: scan_piece1(i, n).wait_send())
        times(1, 8, lambda n, i=i: scan_piece2(i, n).wait_send())
        times(1, 16, lambda n, i=i: scan_piece3(i, n).wait_send())
    rc_copy.wait_send()
    k_store.wait()
    v_store.wait()
    w_store.wait()


def per_device(queries, keys, values, grad_out, out_weight):
    def vmem(*shape, dtype=BF16):
        return pltpu.VMEM(shape, dtype)

    def sems(*shape):
        return [pltpu.SemaphoreType.DMA(shape)] * 2

    wide = (T, T)
    scratch = [
        vmem(*wide), vmem(*wide), vmem(*wide),
        vmem(4, *wide),
        vmem(16, 512),
        vmem(2, 4, 4, 4, 2, 16, 256),
        vmem(*wide, dtype=F32),
        vmem(*wide),
        vmem(*wide, dtype=F32),
        vmem(*wide),
        vmem(*wide, dtype=F32), vmem(*wide, dtype=F32),
        vmem(2, 16, 32, D), vmem(2, 16, 32, D),
        vmem(2, 32, D), vmem(2, 8, 32, D),
        vmem(2, 16, 32, D), vmem(2, 16, 32, D),
        vmem(4, 4, 4, 2, 16, 256, dtype=F32),
        vmem(4, 4, 4, 2, 16, 256),
        vmem(4, 4, 4, 2, 16, 256),
        vmem(4, 4, 4, 2, 16, 256),
        vmem(3, 4, 4, 2, 16, 256),
        vmem(4, 4, 2, 16, 256, dtype=F32),
        vmem(4, 4, 2, 16, 256),
        vmem(3, 4, 2, 16, 256),
        vmem(4, 2, 16, 256, dtype=F32),
        vmem(3, 2, 16, 256, dtype=F32),
        vmem(2, 16, 256, dtype=F32),
        vmem(16, 256, dtype=F32),
        vmem(16, 512, dtype=F32),
        pltpu.SemaphoreType.DMA((5,)), pltpu.SemaphoreType.DMA((4,)),
        *sems(3),
        pltpu.SemaphoreType.DMA, pltpu.SemaphoreType.DMA,
        *sems(3), *sems(3), *sems(3), *sems(4),
        *sems(2, 15), *sems(2, 7), *sems(2, 15),
        *sems(4), *sems(3), *sems(3), *sems(3),
        pltpu.SemaphoreType.DMA, pltpu.SemaphoreType.DMA,
    ]
    shape = jax.ShapeDtypeStruct(wide, BF16)
    return pl.pallas_call(
        kernel,
        out_shape=(shape, shape, shape, jax.ShapeDtypeStruct((16, 512), F32)),
        in_specs=[pl.BlockSpec(memory_space=pl.ANY)] * 5,
        out_specs=[pl.BlockSpec(memory_space=pl.ANY)] * 4,
        scratch_shapes=scratch,
        compiler_params=pltpu.CompilerParams(
            collective_id=0, has_side_effects=True, vmem_limit_bytes=56 * 2**20
        ),
        name="attention_backward",
    )(queries, keys, values, grad_out, out_weight)


def solution(mesh):
    spec = P("seq", "head")
    return jax.shard_map(
        per_device, mesh=mesh, in_specs=(spec,) * 5, out_specs=(spec,) * 4, check_vma=False
    )
```

time: 868 us -> 84.5 us (0.10)
  the two profiles are of different devices: /device:TPU:8 before, /device:TPU:1 now
where the time goes in v1:
time: 84.5 us; the launch traced here: 84.3 us
  Pallas kernels  79 us (93%)
  local copies, waits for them, and re-layouts  4.57 us (5%)
    pallas_call x1, Pallas kernels, per_device(): pl.pallas_call(kernel, out_shape=(shape, shape, shape, jax.ShapeDtypeStru...  79 us
    unnamed x10, local copies, waits for them, and re-layouts  4.57 us

profile of v1, /device:TPU:1, one launch (start us, length us, event | category | flops | bytes accessed | tf_op | source)
XLA Modules:
  0.0 84.3 jit_solution(4327561605890751434)
XLA Ops:
  0.6 79.0 %attention_backward.1 = (bf16[512,512]{1,0:T(8,128)(2,1)}, bf16[512,512]{1,0:T(8,128)(2,1)}, bf16[512,512]{1,0:T(8,128)(2,1)}, f32[16,512]{1,0:T(8,128)}) custom-call(bf16[512,512]{1,0:T(8,128)(2,1)} %q_in.1, bf16[512,512]{1,0:T(8,128)(2,1)} %k_in.1, bf16[512,512]{1,0:T(8,128)(2,1)} %v_in.1, bf16[512,512]{1,0:T(8,128)(2,1)} %g_in.1, bf16[16,512]{1,0:T(8,128)(2,1)} %w_in.1), custom_call_target="tpu_custom_call" | custom-call | tf_op jit(solution)/shard_map/attention_backward/pallas_call | solution.py:446
  79.7 0.0 copy-start.1
  79.7 1.9 %copy.13 = bf16[512,512]{1,0:T(8,128)(2,1)} copy(bf16[512,512]{1,0:T(8,128)(2,1)} %get-tuple-element.8) | data formatting | bytes 1048576
  81.6 0.0 copy-done.1
  81.6 0.0 copy-start
  81.6 0.8 copy.14
  82.4 0.4 copy-done
  82.8 0.0 copy-start.2
  82.8 0.8 copy.15
  83.6 0.0 copy-done.2
  83.6 0.6 copy.16
Async XLA Ops:
  79.7 1.9 %copy-start.1 = (bf16[512,512]{1,0:T(8,128)(2,1)S(1)}, bf16[512,512]{1,0:T(8,128)(2,1)}, u32[]{:S(2)}) copy-start(bf16[512,512]{1,0:T(8,128)(2,1)} %get-tuple-element.9) | copy-start | bytes 1572868
  81.6 1.2 %copy-start = (bf16[512,512]{1,0:T(8,128)(2,1)S(1)}, bf16[512,512]{1,0:T(8,128)(2,1)}, u32[]{:S(2)}) copy-start(bf16[512,512]{1,0:T(8,128)(2,1)} %get-tuple-element.10) | copy-start | bytes 1572868
  82.8 0.8 copy-start.2

commit v2 on v1

v2 whole, which is shorter than its diff:
```python
import math

import jax
import jax.numpy as jnp
from jax import lax
from jax.experimental import pallas as pl
from jax.experimental.pallas import tpu as pltpu
from jax.sharding import PartitionSpec as P

MESH = pl.DeviceIdType.MESH
F32, BF16 = jnp.float32, jnp.bfloat16
D = 128
T = 512
SCALE = 1.0 / math.sqrt(128 * 65536)
WSCALE = 1.0 / math.sqrt(65536)


def dot_nn(a, b):
    return lax.dot_general(a, b, (((1,), (0,)), ((), ())), preferred_element_type=F32)


def dot_nt(a, b):
    return lax.dot_general(a, b, (((1,), (1,)), ((), ())), preferred_element_type=F32)


def dot_tn(a, b):
    return lax.dot_general(a, b, (((0,), (0,)), ((), ())), preferred_element_type=F32)


def heads(body):
    def step(h, carry):
        body(h, pl.ds(pl.multiple_of(h * D, D), D))
        return carry

    lax.fori_loop(0, 4, step, 0)


def each_head(body):
    for h in range(4):
        body(h, slice(h * D, h * D + D))


def times(low, high, body):
    def step(i, carry):
        body(i)
        return carry

    lax.fori_loop(low, high, step, 0)


def kernel(
    q_in, k_in, v_in, g_in, w_in,
    q_out, k_out, v_out, w_out,
    q, k, v, gbuf, gt, qt, wown, wst, av, at, outb, ag, kpart, vpart,
    sb, s1, s2s, s2, s3s, state,
    hf, rs, r1, hb, r2, h2, h2b, r3, h3, ra, rb,
    wo,
    load_sem, store_sem,
    g_ss, g_rs, w0_ss, w0_rs, wa_ss, wa_rs, wb_ss, wb_rs, w2_ss, w2_rs, w3_ss, w3_rs, w4_ss, w4_rs,
    p1_ss, p1_rs, p2_ss, p2_rs, p3_ss, p3_rs,
    r1_ss, r1_rs, r2_ss, r2_rs, r3_ss, r3_rs, ra_ss, ra_rs, rb_ss, rb_rs,
):
    seq = lax.axis_index("seq")
    y = lax.axis_index("head")
    z, x, c = seq // 8, (seq // 2) % 4, seq % 2
    zq, zr = z // 4, z % 4
    group, m = seq // 16, seq % 16
    oc = 1 - c
    a2 = oc * zr + c * x
    a3 = oc * x + c * zr
    zstep = (0, 1, 2, 15, 14)
    hops = ((1, slice(0, 4)), (3, slice(0, 4)), (2, slice(0, 2)), (4, slice(2, 4)))

    def dev(z_, x_, c_):
        return ((z_ * 4 + x_) * 2 + c_, y)

    def along(first, n):
        by_x = (x + (2 if n == 4 else n)) % 4
        return dev(first * ((z + zstep[n]) % 16) + (1 - first) * z, first * x + (1 - first) * by_x, c)

    def peer2(n):
        return along(oc, n)

    def peer3(n):
        return along(c, n)

    def peer4(n, core=c):
        return dev((z + 4 * n) % 16, x, core)

    other = dev(z, x, oc)

    def remote(src, dst, ss, rs_, to):
        return pltpu.make_async_remote_copy(
            src_ref=src, dst_ref=dst, send_sem=ss, recv_sem=rs_, device_id=to, device_id_type=MESH
        )

    loads = [
        pltpu.make_async_copy(src, dst, load_sem.at[i])
        for i, (src, dst) in enumerate(((k_in, k), (v_in, v), (w_in, wown), (q_in, q), (g_in, gbuf.at[y])))
    ]
    for copy in loads:
        copy.start()

    barrier = pltpu.get_barrier_semaphore()

    def greet(to):
        pl.semaphore_signal(barrier, inc=1, device_id=to, device_id_type=MESH)

    times(1, 8, lambda n: greet((((group + n) % 8) * 16 + m, y)))
    times(1, 16, lambda n: greet((group * 16 + (m + n) % 16, y)))
    times(1, 4, lambda n: greet((seq, (y + n) % 4)))
    greet(dev((z + 1) % 16, x, c))
    greet(dev((z + 15) % 16, x, c))
    for n in (1, 2, 3):
        greet(peer4(n, oc))

    own = pl.ds(pl.multiple_of(c * 256, 256), 256)
    others = pl.ds(pl.multiple_of(oc * 256, 256), 256)

    top, bottom = slice(0, 256), slice(256, 512)

    def g_copy(i):
        owner, rows, n = (
            (y, top, 1), (y, bottom, 3), (y, bottom, 1), (y, top, 3),
            ((y + 3) % 4, top, 1), ((y + 1) % 4, bottom, 3),
        )[i]
        part = gbuf.at[owner, rows]
        return remote(part, part, g_ss.at[i], g_rs.at[i], (seq, (y + n) % 4))

    def wa_copy(n):
        return remote(wown.at[:, own], wst.at[c, zq, a3, a2, c], wa_ss.at[n - 1], wa_rs.at[n - 1], peer4(n))

    def wb_copy(n):
        return remote(wown.at[:, others], wst.at[oc, zq, a2, a3, c], wb_ss.at[n - 1], wb_rs.at[n - 1], peer4(n, oc))

    w0 = remote(wown.at[:, others], wst.at[oc, zq, a2, a3, c], w0_ss, w0_rs, other)

    def scan_piece1(i, n):
        to = (m + n) % 16
        return remote(sb.at[i, to], s1.at[i, m], p1_ss.at[i, n - 1], p1_rs.at[i, n - 1], (group * 16 + to, y))

    def scan_piece2(i, n):
        return remote(s2s.at[i], s2.at[i, group], p2_ss.at[i, n - 1], p2_rs.at[i, n - 1], (((group + n) % 8) * 16 + m, y))

    def scan_piece3(i, n):
        to = (m + n) % 16
        return remote(s3s.at[i, to], state.at[i, m], p3_ss.at[i, n - 1], p3_rs.at[i, n - 1], (group * 16 + to, y))

    def scan_own(i, product):
        def one(h, cols):
            s = product(cols).astype(BF16)
            sb[i, h * 4 : h * 4 + 4] = s.reshape(4, 32, D)

        each_head(one)
        s1[i, m] = sb[i, m]

    def scan_start(i):
        times(1, 16, lambda n: scan_piece1(i, n).start())

    def scan_total(i):
        times(1, 16, lambda n: scan_piece1(i, n).wait_recv())
        total = s1[i, 0].astype(F32)
        for j in range(1, 16):
            total += s1[i, j].astype(F32)
        s2s[i] = total.astype(s2s.dtype)
        times(1, 8, lambda n: scan_piece2(i, n).start())
        s2[i, group] = jnp.zeros_like(s2[i, group])

    def scan_back(i):
        times(1, 8, lambda n: scan_piece2(i, n).wait_recv())
        run = jnp.zeros((32, D), F32)
        for j in range(8):
            counts = (j < group) if i == 0 else (j > group)
            run += jnp.where(counts, s2[i, j].astype(F32), 0.0)
        for j in range(16) if i == 0 else range(15, -1, -1):
            s3s[i, j] = run.astype(BF16)
            run += s1[i, j].astype(F32)
        times(1, 16, lambda n: scan_piece3(i, n).start())
        state[i, m] = s3s[i, m]

    def scan_get(i):
        times(1, 16, lambda n: scan_piece3(i, n).wait_recv())

    def state_of(i, h):
        return state[i, pl.ds(h * 4, 4)].reshape(D, D)

    loads[0].wait()
    loads[1].wait()
    scan_own(0, lambda cols: dot_tn(k[:, cols], v[:, cols]))
    loads[2].wait()
    wst[c, zq, a3, a2, c] = wown[:, own]

    pl.semaphore_wait(barrier, 30)

    for n in (2, 1, 3):
        wa_copy(n).start()
        wb_copy(n).start()
    w0.start()
    scan_start(0)
    loads[4].wait()
    for i in range(4):
        g_copy(i).start()
    loads[3].wait()

    def lower(n, height):
        row = lax.broadcasted_iota(jnp.int32, (D, n), 0) + height
        col = lax.broadcasted_iota(jnp.int32, (D, n), 1)
        return row >= col

    def upper(n):
        row = lax.broadcasted_iota(jnp.int32, (D, n), 0)
        col = lax.broadcasted_iota(jnp.int32, (D, n), 1)
        return col >= row

    def attend(h, cols):
        for r in range(4):
            n = (r + 1) * D
            rows = slice(r * D, n)
            s = dot_nt(q[rows, cols], k[:n, cols])
            s = jnp.where(lower(n, r * D), s, 0.0).astype(BF16)
            av[rows, cols] = dot_nn(s, v[:n, cols])

    heads(attend)

    scan_total(0)

    for i in range(2):
        g_copy(i).wait_recv()
        g_copy(i + 4).start()

    def w2_copy(n, zs):
        part = wst.at[c, zs, a3, a2]
        return remote(part, part, w2_ss.at[n - 1], w2_rs.at[n - 1], peer2(n))

    def w3_copy(d, n, zs):
        part = wst.at[c, zs, a3, (a2 + d) % 4]
        return remote(part, part, w3_ss.at[d, n - 1], w3_rs.at[d, n - 1], peer3(n))

    def w4_copy(d, e):
        part = wst.at[c, :, (a3 + e) % 4, (a2 + d) % 4]
        return remote(part, part, w4_ss.at[d, e], w4_rs.at[d, e], other)

    def w3_start(d):
        for n, zs in hops:
            w3_copy(d, n, zs).start()
        w4_copy(d, 0).start()

    w0.wait_recv()
    for n in (1, 3, 2):
        wa_copy(n).wait_recv()
        wb_copy(n).wait_recv()
    for n, zs in hops:
        w2_copy(n, zs).start()
    w3_start(0)
    qt[...] = q[...].T
    gt[y] = gbuf[y].T
    for n, zs in hops:
        w2_copy(n, zs).wait_recv()
        if n != 2:
            w3_start(4 - n or 2)

    def attend_t(h, cols):
        for r in range(4):
            rows = slice(r * D, (r + 1) * D)
            s = dot_nt(k[rows, cols], q[r * D :, cols])
            at[h, rows, r * D :] = jnp.where(upper(T - r * D), s, 0.0).astype(BF16)

    heads(attend_t)

    scan_back(0)

    for d in (0, 3, 1, 2):
        for n, zs in hops:
            w3_copy(d, n, zs).wait_recv()
            if n != 2:
                w4_copy(d, 4 - n or 2).start()

    for i in range(2, 6):
        g_copy(i).wait_recv()
    for n in (1, 3, 2):
        gt[(y + n) % 4] = gbuf[(y + n) % 4].T

    scan_get(0)

    def rec(h, cols):
        outb[:, cols] = (SCALE * (av[:, cols] + dot_nn(q[:, cols], state_of(0, h)))).astype(BF16)

    each_head(rec)

    def r1_copy(i):
        return remote(rs.at[i], r1.at[i], r1_ss.at[i], r1_rs.at[i], other)

    def contribute(i):
        mine = dot_nn(gt[i], outb[:, own])
        theirs = dot_nn(gt[i], outb[:, others])
        for zi in range(4):
            for xi in range(4):
                rows = slice((zi * 4 + xi) * 32, (zi * 4 + xi) * 32 + 32)
                of_x, of_z = oc * xi + c * zi, oc * zi + c * xi
                hf[i, of_x, of_z] = mine[rows].reshape(2, 16, 256)
                rs[i, of_z, of_x] = theirs[rows].reshape(2, 16, 256).astype(BF16)
        r1_copy(i).start()

    times(0, 4, contribute)

    def project(half, cols):
        first = 1 - half
        total = None
        for i in range(4):
            w = [
                wst[half, i, first * xi + half * zi, first * zi + half * xi].reshape(32, 256)
                for zi in range(4)
                for xi in range(4)
            ]
            part = dot_nn(gbuf[i], jnp.concatenate(w, axis=0))
            total = part if total is None else total + part
        ag[:, cols] = total.astype(BF16)

    project(c, own)
    for d in range(4):
        for e in range(4):
            w4_copy(d, e).wait_recv()
    project(oc, others)

    scan_own(1, lambda cols: dot_nn(qt[cols], ag[:, cols]))
    scan_start(1)

    def r2_copy(p, d, n):
        to = peer3(4 if n == 2 and p == 1 else n)
        part = (a2 + d) % 4
        zs = slice(2 * p, 2 * p + 2)
        return remote(
            hb.at[n - 1, part, zs], r2.at[n - 1, part, zs], r2_ss.at[p, d, n - 1], r2_rs.at[p, d, n - 1], to
        )

    for p in range(2):
        for i in (2 * p, 2 * p + 1):
            r1_copy(i).wait_recv()
            for n in (1, 3, 2):
                u = (a3 + n) % 4
                hb[n - 1, :, i] = (hf[i, u] + r1[i, u].astype(F32)).astype(BF16)
            h2[:, i] = hf[i, a3] + r1[i, a3].astype(F32)
        for d in (1, 3, 2, 0):
            for n in (1, 3, 2):
                r2_copy(p, d, n).start()

    def back(h, cols):
        for r in range(4):
            n = (r + 1) * D
            rows = slice(r * D, n)
            s = dot_nt(ag[rows, cols], v[:n, cols])
            s = jnp.where(lower(n, r * D), s, 0.0).astype(BF16)
            total = dot_nn(s, k[:n, cols]) + dot_nt(ag[rows, cols], state_of(0, h))
            outb[rows, cols] = (SCALE * total).astype(BF16)

    def back_kv(h, cols):
        for r in range(4):
            rows = slice(r * D, (r + 1) * D)
            mask = upper(T - r * D)
            s = dot_nt(v[rows, cols], ag[r * D :, cols])
            s = jnp.where(mask, s, 0.0).astype(BF16)
            kpart[rows, cols] = dot_nn(s, q[r * D :, cols])
            vpart[rows, cols] = dot_nn(at[h, rows, r * D :], ag[r * D :, cols])

    heads(back)
    q_store = pltpu.make_async_copy(outb, q_out, store_sem.at[0])
    q_store.start()
    scan_total(1)
    heads(back_kv)

    def r3_copy(n, zs):
        slot = (n if n < 4 else 2) - 1
        return remote(h2b.at[slot, zs], r3.at[slot, zs], r3_ss.at[n - 1], r3_rs.at[n - 1], peer2(n))

    for d in (1, 3, 2, 0):
        part = (a2 + d) % 4
        total = h2[part]
        for n in (1, 3, 2):
            for p in range(2):
                r2_copy(p, d, n).wait_recv()
            total += r2[n - 1, part].astype(F32)
        if d:
            h2b[d - 1] = total.astype(BF16)
            for n, zs in hops:
                if n == d or n == d + 2 == 4:
                    r3_copy(n, zs).start()
        else:
            h2[part] = total

    scan_back(1)

    def ra_copy(n):
        return remote(h3.at[(zq + n) % 4, c], ra.at[n - 1], ra_ss.at[n - 1], ra_rs.at[n - 1], peer4(n))

    def rb_copy(n):
        return remote(h3.at[(zq + n) % 4, oc], rb.at[n], rb_ss.at[n], rb_rs.at[n], peer4(n, oc) if n else other)

    for n, zs in hops:
        r3_copy(n, zs).wait_recv()
    for i in range(4):
        total = h2[a2, i]
        for n in range(3):
            total += r3[n, i].astype(F32)
        h3[i] = total
    for n in (2, 1, 3):
        ra_copy(n).start()
        rb_copy(n).start()
    rb_copy(0).start()

    scan_get(1)

    q_store.wait()

    def final_k(h, cols):
        outb[:, cols] = (SCALE * (kpart[:, cols] + dot_nt(v[:, cols], state_of(1, h)))).astype(BF16)

    def final_v(h, cols):
        ag[:, cols] = (SCALE * (vpart[:, cols] + dot_nn(k[:, cols], state_of(1, h)))).astype(BF16)

    k_store = pltpu.make_async_copy(outb, k_out, store_sem.at[1])
    v_store = pltpu.make_async_copy(ag, v_out, store_sem.at[2])
    each_head(final_k)
    k_store.start()
    each_head(final_v)
    v_store.start()

    mine = h3[zq, c]
    for n in range(3):
        ra_copy(n + 1).wait_recv()
        mine += ra[n]
    wo[:, own] = mine * WSCALE
    rb_copy(0).wait_recv()
    theirs = rb[0]
    for n in range(1, 4):
        rb_copy(n).wait_recv()
        theirs += rb[n]
    wo[:, others] = theirs * WSCALE
    w_store = pltpu.make_async_copy(wo, w_out, store_sem.at[3])
    w_store.start()

    w0.wait_send()
    for n, zs in hops:
        w2_copy(n, zs).wait_send()
        r3_copy(n, zs).wait_send()
        for d in range(4):
            w3_copy(d, n, zs).wait_send()
    for n in (1, 2, 3):
        wa_copy(n).wait_send()
        wb_copy(n).wait_send()
        ra_copy(n).wait_send()
    for n in range(4):
        rb_copy(n).wait_send()
        r1_copy(n).wait_send()
        for d in range(4):
            w4_copy(d, n).wait_send()
    for p in range(2):
        for d in range(4):
            for n in (1, 2, 3):
                r2_copy(p, d, n).wait_send()
    for i in range(6):
        g_copy(i).wait_send()
    for i in range(2):
        times(1, 16, lambda n, i=i: scan_piece1(i, n).wait_send())
        times(1, 8, lambda n, i=i: scan_piece2(i, n).wait_send())
        times(1, 16, lambda n, i=i: scan_piece3(i, n).wait_send())
    k_store.wait()
    v_store.wait()
    w_store.wait()


def hand_over(*refs):
    ins, outs, held, sem = refs[:4], refs[4:8], refs[8:12], refs[12]
    reads = [pltpu.make_async_copy(ins[i], held[i], sem.at[0, i]) for i in range(4)]
    writes = [pltpu.make_async_copy(held[i], outs[i], sem.at[1, i]) for i in range(4)]
    for read in reads:
        read.start()
    for read, write in zip(reads, writes):
        read.wait()
        write.start()
    for write in writes:
        write.wait()


def per_device(queries, keys, values, grad_out, out_weight):
    def vmem(*shape, dtype=BF16):
        return pltpu.VMEM(shape, dtype)

    def sems(*shape):
        return [pltpu.SemaphoreType.DMA(shape)] * 2

    wide = (T, T)
    scratch = [
        vmem(*wide), vmem(*wide), vmem(*wide),
        vmem(4, *wide), vmem(4, *wide), vmem(*wide),
        vmem(16, 512),
        vmem(2, 4, 4, 4, 2, 16, 256),
        vmem(*wide, dtype=F32),
        vmem(4, *wide),
        vmem(*wide),
        vmem(*wide),
        vmem(*wide, dtype=F32), vmem(*wide, dtype=F32),
        vmem(2, 16, 32, D), vmem(2, 16, 32, D),
        vmem(2, 32, D), vmem(2, 8, 32, D),
        vmem(2, 16, 32, D), vmem(2, 16, 32, D),
        vmem(4, 4, 4, 2, 16, 256, dtype=F32),
        vmem(4, 4, 4, 2, 16, 256),
        vmem(4, 4, 4, 2, 16, 256),
        vmem(3, 4, 4, 2, 16, 256),
        vmem(3, 4, 4, 2, 16, 256),
        vmem(4, 4, 2, 16, 256, dtype=F32),
        vmem(3, 4, 2, 16, 256),
        vmem(3, 4, 2, 16, 256),
        vmem(4, 2, 16, 256, dtype=F32),
        vmem(3, 16, 256, dtype=F32),
        vmem(4, 16, 256, dtype=F32),
        vmem(16, 512, dtype=F32),
        pltpu.SemaphoreType.DMA((5,)), pltpu.SemaphoreType.DMA((4,)),
        *sems(6),
        pltpu.SemaphoreType.DMA, pltpu.SemaphoreType.DMA,
        *sems(3), *sems(3), *sems(4), *sems(4, 4), *sems(4, 4),
        *sems(2, 15), *sems(2, 7), *sems(2, 15),
        *sems(4), *sems(2, 4, 3), *sems(4), *sems(3), *sems(4),
    ]
    shape = jax.ShapeDtypeStruct(wide, BF16)
    outs = pl.pallas_call(
        kernel,
        out_shape=(shape, shape, shape, jax.ShapeDtypeStruct((16, 512), F32)),
        in_specs=[pl.BlockSpec(memory_space=pl.ANY)] * 5,
        out_specs=[pl.BlockSpec(memory_space=pl.ANY)] * 4,
        scratch_shapes=scratch,
        compiler_params=pltpu.CompilerParams(
            collective_id=0, has_side_effects=True, vmem_limit_bytes=56 * 2**20
        ),
        name="attention_backward",
    )(queries, keys, values, grad_out, out_weight)
    return pl.pallas_call(
        hand_over,
        out_shape=tuple(jax.ShapeDtypeStruct(a.shape, a.dtype) for a in outs),
        in_specs=[pl.BlockSpec(memory_space=pl.ANY)] * 4,
        out_specs=[pl.BlockSpec(memory_space=pl.ANY)] * 4,
        scratch_shapes=[vmem(*a.shape, dtype=a.dtype) for a in outs] + [pltpu.SemaphoreType.DMA((2, 4))],
        name="hand_over",
    )(*outs)


def solution(mesh):
    spec = P("seq", "head")
    return jax.shard_map(
        per_device, mesh=mesh, in_specs=(spec,) * 5, out_specs=(spec,) * 4, check_vma=False
    )
```

time: 84.5 us -> 76.1 us (0.901)
  local copies, waits for them, and re-layouts: 4.57 us -> 0 us
  Pallas kernels: 79 us -> 75.3 us
    pallas_call x1, Pallas kernels: 79 us -> 73 us  [per_device(): pl.pallas_call(kernel, out_shape=(shape, shape, shape, jax.ShapeDtypeStru...]
    unnamed x10 -> x0, local copies, waits for them, and re-layouts: 4.57 us -> none
    pallas_call x0 -> x1, Pallas kernels: none -> 2.25 us  [per_device(): pl.pallas_call(hand_over, out_shape=tuple((jax.ShapeDtypeStruct(a.shape,...]
where the time goes in v2:
time: 76.1 us; the launch traced here: 75.9 us
  Pallas kernels  75.3 us (99%)
    pallas_call x1, Pallas kernels, per_device(): pl.pallas_call(kernel, out_shape=(shape, shape, shape, jax.ShapeDtypeStru...  73 us
    pallas_call x1, Pallas kernels, per_device(): pl.pallas_call(hand_over, out_shape=tuple((jax.ShapeDtypeStruct(a.shape,...  2.25 us

profile of v2, /device:TPU:1, one launch (start us, length us, event | category | flops | bytes accessed | tf_op | source)
XLA Modules:
  0.0 75.9 jit_solution(12227369992311164821)
XLA Ops:
  0.6 73.0 %attention_backward.1 = (bf16[512,512]{1,0:T(8,128)(2,1)}, bf16[512,512]{1,0:T(8,128)(2,1)}, bf16[512,512]{1,0:T(8,128)(2,1)}, f32[16,512]{1,0:T(8,128)}) custom-call(bf16[512,512]{1,0:T(8,128)(2,1)} %q_in.1, bf16[512,512]{1,0:T(8,128)(2,1)} %k_in.1, bf16[512,512]{1,0:T(8,128)(2,1)} %v_in.1, bf16[512,512]{1,0:T(8,128)(2,1)} %g_in.1, bf16[16,512]{1,0:T(8,128)(2,1)} %w_in.1), custom_call_target="tpu_custom_call" | custom-call | tf_op jit(solution)/shard_map/attention_backward/pallas_call | solution.py:525
  73.7 2.3 %hand_over.1 = (bf16[512,512]{1,0:T(8,128)(2,1)}, bf16[512,512]{1,0:T(8,128)(2,1)}, bf16[512,512]{1,0:T(8,128)(2,1)}, f32[16,512]{1,0:T(8,128)}) custom-call(bf16[512,512]{1,0:T(8,128)(2,1)} %get-tuple-element.8.refs_0_, bf16[512,512]{1,0:T(8,128)(2,1)} %get-tuple-element.9.refs_1_, bf16[512,512]{1,0:T(8,128)(2,1)} %get-tuple-element.10.refs_2_, ...), custom_call_target="tpu_custom_call" | custom-call | tf_op jit(solution)/shard_map/hand_over/pallas_call | solution.py:536

commit v3 on v2

--- a/solution.py
+++ b/solution.py
@@ -192,11 +192,11 @@
 
     pl.semaphore_wait(barrier, 30)
 
+    scan_start(0)
     for n in (2, 1, 3):
         wa_copy(n).start()
         wb_copy(n).start()
     w0.start()
-    scan_start(0)
     loads[4].wait()
     for i in range(4):
         g_copy(i).start()
@@ -265,15 +265,8 @@
             s = dot_nt(k[rows, cols], q[r * D :, cols])
             at[h, rows, r * D :] = jnp.where(upper(T - r * D), s, 0.0).astype(BF16)
 
+    scan_back(0)
     heads(attend_t)
-
-    scan_back(0)
-
-    for d in (0, 3, 1, 2):
-        for n, zs in hops:
-            w3_copy(d, n, zs).wait_recv()
-            if n != 2:
-                w4_copy(d, 4 - n or 2).start()
 
     for i in range(2, 6):
         g_copy(i).wait_recv()
@@ -301,7 +294,33 @@
                 rs[i, of_z, of_x] = theirs[rows].reshape(2, 16, 256).astype(BF16)
         r1_copy(i).start()
 
-    times(0, 4, contribute)
+    for i, d in enumerate((0, 3, 1, 2)):
+        contribute(i)
+        for n, zs in hops:
+            w3_copy(d, n, zs).wait_recv()
+            if n != 2:
+                w4_copy(d, 4 - n or 2).start()
+
+    def r2_copy(p, d, n):
+        to = peer3(4 if n == 2 and p == 1 else n)
+        part = (a2 + d) % 4
+        zs = slice(2 * p, 2 * p + 2)
+        return remote(
+            hb.at[n - 1, part, zs], r2.at[n - 1, part, zs], r2_ss.at[p, d, n - 1], r2_rs.at[p, d, n - 1], to
+        )
+
+    def pair(p):
+        for i in (2 * p, 2 * p + 1):
+            r1_copy(i).wait_recv()
+            for n in (1, 3, 2):
+                u = (a3 + n) % 4
+                hb[n - 1, :, i] = (hf[i, u] + r1[i, u].astype(F32)).astype(BF16)
+            h2[:, i] = hf[i, a3] + r1[i, a3].astype(F32)
+        for d in (1, 3, 2, 0):
+            for n in (1, 3, 2):
+                r2_copy(p, d, n).start()
+
+    pair(0)
 
     def project(half, cols):
         first = 1 - half
@@ -325,24 +344,7 @@
     scan_own(1, lambda cols: dot_nn(qt[cols], ag[:, cols]))
     scan_start(1)
 
-    def r2_copy(p, d, n):
-        to = peer3(4 if n == 2 and p == 1 else n)
-        part = (a2 + d) % 4
-        zs = slice(2 * p, 2 * p + 2)
-        return remote(
-            hb.at[n - 1, part, zs], r2.at[n - 1, part, zs], r2_ss.at[p, d, n - 1], r2_rs.at[p, d, n - 1], to
-        )
-
-    for p in range(2):
-        for i in (2 * p, 2 * p + 1):
-            r1_copy(i).wait_recv()
-            for n in (1, 3, 2):
-                u = (a3 + n) % 4
-                hb[n - 1, :, i] = (hf[i, u] + r1[i, u].astype(F32)).astype(BF16)
-            h2[:, i] = hf[i, a3] + r1[i, a3].astype(F32)
-        for d in (1, 3, 2, 0):
-            for n in (1, 3, 2):
-                r2_copy(p, d, n).start()
+    pair(1)
 
     def back(h, cols):
         for r in range(4):
@@ -366,7 +368,6 @@
     q_store = pltpu.make_async_copy(outb, q_out, store_sem.at[0])
     q_store.start()
     scan_total(1)
-    heads(back_kv)
 
     def r3_copy(n, zs):
         slot = (n if n < 4 else 2) - 1
@@ -387,13 +388,13 @@
         else:
             h2[part] = total
 
-    scan_back(1)
-
     def ra_copy(n):
         return remote(h3.at[(zq + n) % 4, c], ra.at[n - 1], ra_ss.at[n - 1], ra_rs.at[n - 1], peer4(n))
 
     def rb_copy(n):
         return remote(h3.at[(zq + n) % 4, oc], rb.at[n], rb_ss.at[n], rb_rs.at[n], peer4(n, oc) if n else other)
+
+    heads(back_kv)
 
     for n, zs in hops:
         r3_copy(n, zs).wait_recv()
@@ -406,6 +407,8 @@
         ra_copy(n).start()
         rb_copy(n).start()
     rb_copy(0).start()
+
+    scan_back(1)
 
     scan_get(1)
 

time: 76.1 us -> 73.3 us (0.963)
  Pallas kernels: 75.3 us -> 72 us
    pallas_call x1, Pallas kernels: 73 us -> 69.8 us  [per_device(): pl.pallas_call(kernel, out_shape=(shape, shape, shape, jax.ShapeDtypeStru...]
where the time goes in v3:
time: 73.3 us; the launch traced here: 72.6 us
  Pallas kernels  72 us (98%)
    pallas_call x1, Pallas kernels, per_device(): pl.pallas_call(kernel, out_shape=(shape, shape, shape, jax.ShapeDtypeStru...  69.8 us
    pallas_call x1, Pallas kernels, per_device(): pl.pallas_call(hand_over, out_shape=tuple((jax.ShapeDtypeStruct(a.shape,...  2.25 us

profile of v3, /device:TPU:1, one launch (start us, length us, event | category | flops | bytes accessed | tf_op | source)
XLA Modules:
  0.0 72.6 jit_solution(1680925069040105346)
XLA Ops:
  0.6 69.8 %attention_backward.1 = (bf16[512,512]{1,0:T(8,128)(2,1)}, bf16[512,512]{1,0:T(8,128)(2,1)}, bf16[512,512]{1,0:T(8,128)(2,1)}, f32[16,512]{1,0:T(8,128)}) custom-call(bf16[512,512]{1,0:T(8,128)(2,1)} %q_in.1, bf16[512,512]{1,0:T(8,128)(2,1)} %k_in.1, bf16[512,512]{1,0:T(8,128)(2,1)} %v_in.1, bf16[512,512]{1,0:T(8,128)(2,1)} %g_in.1, bf16[16,512]{1,0:T(8,128)(2,1)} %w_in.1), custom_call_target="tpu_custom_call" | custom-call | tf_op jit(solution)/shard_map/attention_backward/pallas_call | solution.py:528
  70.4 2.3 %hand_over.1 = (bf16[512,512]{1,0:T(8,128)(2,1)}, bf16[512,512]{1,0:T(8,128)(2,1)}, bf16[512,512]{1,0:T(8,128)(2,1)}, f32[16,512]{1,0:T(8,128)}) custom-call(bf16[512,512]{1,0:T(8,128)(2,1)} %get-tuple-element.8.refs_0_, bf16[512,512]{1,0:T(8,128)(2,1)} %get-tuple-element.9.refs_1_, bf16[512,512]{1,0:T(8,128)(2,1)} %get-tuple-element.10.refs_2_, ...), custom_call_target="tpu_custom_call" | custom-call | tf_op jit(solution)/shard_map/hand_over/pallas_call | solution.py:539
